TPU v7x, 32 devices: a whole 2x2x4 slice. The times are simulated.
32 devices in a mesh: grp: 4 (over z), dev: 8 (over y, x, core).
Axes of the slice: x: 2, y: 2, z: 4, core: 2. Of those that a mesh axis runs over, the one named last changes fastest.
Arguments:
- points: float32 [3, 524288], P(None, ('grp', 'dev')), may hold values from -6 to 6
- rhs: float32 [32, 524288], P(None, ('grp', 'dev')), may hold values from -6 to 6
- leaf_count: int32 [2048], P(('grp', 'dev')), may hold values from 64 to 256
- near_list: int32 [2048, 8], P(('grp', 'dev')), may hold values from 0 to 2047, as said below
- leaf_basis: float32 [64, 524288], P(None, ('grp', 'dev')), may hold values from -0.375 to 0.375
- leaf_transfer: float32 [64, 131072], P(None, ('grp', 'dev')), may hold values from -0.75 to 0.75
- leaf_parent: int32 [2048], P(('grp', 'dev')), may hold values from 0 to 255, as said below
- nodes1: float32 [3, 16384], P(None, ('grp', 'dev')), may hold values from -6 to 6
- box_transfer: float32 [64, 16384], P(None, ('grp', 'dev')), may hold values from -0.75 to 0.75
- box_parent: int32 [256], P(('grp', 'dev')), may hold values from 0 to 31, as said below
- far1: int32 [256, 16], P(('grp', 'dev')), may hold values from 0 to 255, as said below
- nodes2: float32 [3, 2048], replicated, may hold values from -6 to 6
- far2: int32 [32, 8], replicated, may hold values from 0 to 31, as said below
Outputs:
- result: float32 [32, 524288], P(None, ('grp', 'dev'))
Inputs may be any that keep to these rules, and one draw needn't show every extreme that they name: `near_list`: row c begins with c itself; its other 7 entries are distinct leaf blocks of the same group of 512 blocks (c // 512 alike), each different from c by at most 32. `leaf_parent`: leaf c's box lies on the same device: it is one of boxes (c // 64) * 8 to (c // 64 + 1) * 8 - 1, and every box has exactly 8 leaves. `box_parent`: box b's parent belongs to its group: it is one of (b // 64) * 8 to (b // 64 + 1) * 8 - 1, and every level-2 box has exactly 8 children. `far1`: row t names 16 distinct level-1 boxes of t's group (b // 64 alike), never t. `far2`: row t names 8 distinct level-2 boxes, never t.
All inputs are finite; a program needn't handle non-finite values.
Results may differ from a plain program's by a relative error of at most 0.00011.
Values sent between devices are 32-bit elements; how exact they have to be, the bound alone decides.
No kernel may reach another device: no remote copies, remote signals or barrier semaphores. Data moves between devices by JAX's collectives and lax.ppermute only.
A program may use at most 128 MiB of HBM per device.

v0:
```python
import jax
import jax.numpy as jnp
from jax import lax
from jax.experimental import pallas as pl
from jax.experimental.pallas import tpu as pltpu
from jax.sharding import PartitionSpec as P

B = 256
K = 64
R = 32
NEAR = 8
CHILD = 8
REACH = 32
ROWS = 16
PER = B // ROWS
UNROLL = 8
SPAN = NEAR * PER + PER

F32 = jnp.float32
BF16 = jnp.bfloat16
HIGH = lax.Precision.HIGHEST
LIMIT = 58 * 1024 * 1024

PIECES = ((0, 0), (0, 1), (1, 0), (1, 1), (0, 2), (2, 0), (1, 2), (2, 1))


def params():
    return pltpu.CompilerParams(vmem_limit_bytes=LIMIT)


def vmem():
    return pl.BlockSpec(memory_space=pltpu.VMEM)


def smem():
    return pl.BlockSpec(memory_space=pltpu.SMEM)


def split(x):
    high = x.astype(BF16)
    return high, (x - high.astype(F32)).astype(BF16)


def to_grid(x, step):
    big = 1.5 * 2.0**23 * step
    return (x + big) - big


def dot(a, b):
    return jnp.dot(a, b, preferred_element_type=F32)


def dot_nt(a, b):
    return lax.dot_general(a, b, (((1,), (1,)), ((), ())), preferred_element_type=F32)


def features(coords, targets=True):
    n = coords.shape[1]
    scaled = jnp.concatenate([coords * 4.0, jnp.zeros((5, n), F32)], axis=0)
    one = to_grid(scaled, 2.0**-3)
    rest = scaled - one
    two = to_grid(rest, 2.0**-11)
    three = rest - two
    pieces = (one, two, three)
    square = jnp.sum(one * one, axis=0, keepdims=True)
    s_one = to_grid(square, 8.0)
    s_two = square - s_one
    tail = jnp.sum(rest * (scaled + one), axis=0, keepdims=True)
    q_one = to_grid(tail, 2.0**-4)
    tail = tail - q_one
    q_two = to_grid(tail, 2.0**-12)
    norms = (s_one, s_two, q_one, q_two, tail - q_two)
    row = lax.broadcasted_iota(jnp.int32, (8, n), 0)
    sources, wanted = [], []
    for at, (first, second) in enumerate(PIECES):
        src = pieces[first]
        tgt = pieces[second] * -2.0
        if at < 5:
            src = jnp.where(row == 3, norms[at], jnp.where(row == 4, 1.0, src))
            tgt = jnp.where(row == 3, 1.0, jnp.where(row == 4, norms[at], tgt))
        elif at == 5:
            src = jnp.where(row == 3, 1.0, src)
            tgt = jnp.where(row == 3, 1.0, tgt)
        sources.append(src)
        wanted.append(tgt)
    source = jnp.concatenate(sources, axis=0).astype(BF16)
    if not targets:
        return source, None
    return source, jnp.concatenate(wanted, axis=0).astype(BF16)


def masked(x, count):
    slot = lax.broadcasted_iota(jnp.int32, x.shape, 1)
    return jnp.where(slot < count, x, 0.0)


def null_rows(table, start):
    source, _ = features(jnp.zeros((3, B), F32), False)
    rows = jnp.concatenate([source, jnp.zeros((2 * R, B), BF16)], axis=0).T
    table[start : start + ROWS, :] = rows[:ROWS, :]


def upward(boxes, coarse, group_of, points, rhs, basis, transfer, nodes, lower, counts, parents, uppers, offset, table, wanted, sent, left, right, top):
    del group_of
    leaves = points.shape[1] // B
    left[...] = jnp.zeros_like(left)
    right[...] = jnp.zeros_like(right)
    top[...] = jnp.zeros_like(top)
    null_rows(table, leaves * B)

    def pair(at):
        rows = []
        for side in range(2):
            c = at * 2 + side
            where = pl.ds(pl.multiple_of(c * B, B), B)
            x = masked(rhs[:, where], counts[c])
            x_two = jnp.concatenate(split(x), axis=0)
            source, target = features(points[:, where])
            wanted[c] = target
            table[where, :] = jnp.concatenate([source, x_two], axis=0).T
            b_two = jnp.concatenate(split(basis[:, where]), axis=0)
            r = dot_nt(x_two, b_two)
            rows.append(r[:R, :K] + r[:R, K:] + r[R:, :K])
        m = jnp.concatenate(rows, axis=0)
        high, low = split(m)
        left_side = jnp.concatenate(
            [jnp.concatenate([high, high], axis=1), jnp.concatenate([low, low], axis=1)], axis=0
        )
        e_two = jnp.concatenate(split(transfer[:, pl.ds(pl.multiple_of(at * 2 * K, 2 * K), 2 * K)]), axis=0)
        lifted = dot(left_side, e_two)
        lifted = lifted[: 2 * R] + lifted[2 * R :]
        p_zero = parents[at * 2] - offset[0]
        p_one = parents[at * 2 + 1] - offset[0]
        left[p_zero] += lifted[:R]
        right[p_one] += lifted[R:]

    group = 4

    def step(i, carry):
        for q in range(group):
            pair(i * group + q)
        return carry

    lax.fori_loop(0, leaves // 2 // group, step, 0)
    m_one = [left[b][:, :K] + right[b][:, K:] for b in range(boxes)]
    for b in range(boxes):
        f = lower[:, (b // 2) * 2 * K : (b // 2 + 1) * 2 * K]
        raised = jnp.dot(m_one[b], f, precision=HIGH, preferred_element_type=F32)
        raised = raised[:, (b % 2) * K : (b % 2 + 1) * K]
        top[uppers[b] - offset[1]] += raised
    zero = jnp.zeros((8, sent.shape[1]), F32)
    sent[K : K + 8, :] = zero
    sent[K : K + 3, : boxes * K] = nodes[...]
    for q in range(boxes // 4):
        block = jnp.concatenate(m_one[4 * q : 4 * q + 4], axis=0)
        sent[:K, q * 4 * R : (q + 1) * 4 * R] = block.T
    for q in range(coarse // 4):
        block = jnp.concatenate([top[4 * q + z] for z in range(4)], axis=0)
        sent[:K, (boxes + 4 * q) * R : (boxes + 4 * q + 4) * R] = block.T


def near_items(items, rows_of, table, wanted, out, kept, highs, lows, total):
    def first(t, s):
        code = items[t]
        c = code // 16
        base = (code % 16) * PER
        rows = jnp.concatenate(
            [table[pl.ds(pl.multiple_of(rows_of[c, base + q], ROWS), ROWS), :] for q in range(PER)], axis=0
        )
        kept[s][...] = rows
        u = dot(rows[:, :K], wanted[c])
        high, low = split(lax.rsqrt(u))
        highs[s][...] = high
        lows[s][...] = low

    def second(t, s):
        c = items[t] // 16
        x = kept[s][...].T[K:]
        a = dot(x, highs[s][...])
        b = dot(x[:R], lows[s][...])
        out[c] += a[:R] + a[R:] + b

    groups = (total + UNROLL - 1) // UNROLL

    @pl.when(groups > 0)
    def _():
        for q in range(UNROLL):
            first(q, q)

        def step(g, carry):
            for q in range(UNROLL):
                second((g - 1) * UNROLL + q, q)
                first(g * UNROLL + q, q)
            return carry

        lax.fori_loop(1, groups, step, 0)
        for q in range(UNROLL):
            second((groups - 1) * UNROLL + q, q)


def near_own(items, rows_of, total, table, wanted, out, *scratch):
    kept, highs, lows = scratch[:UNROLL], scratch[UNROLL : 2 * UNROLL], scratch[2 * UNROLL :]
    out[...] = jnp.zeros_like(out)
    near_items(items, rows_of, table, wanted, out, kept, highs, lows, total[0])


def near_halo(items, rows_of, total, counts, before, after, wanted, begun, out, table, *scratch):
    kept, highs, lows = scratch[:UNROLL], scratch[UNROLL : 2 * UNROLL], scratch[2 * UNROLL :]
    null_rows(table, 2 * REACH * B)
    out[...] = begun[...]

    for part, data in ((0, before), (1, after)):

        def step(i, carry, part=part, data=data):
            for q in range(4):
                c = i * 4 + q
                where = pl.ds(pl.multiple_of(c * B, B), B)
                x = masked(data[:R, where], counts[part * REACH + c])
                source, _ = features(data[R : R + 3, where], False)
                to = pl.ds(pl.multiple_of((part * REACH + c) * B, B), B)
                table[to, :] = jnp.concatenate([source, *split(x)], axis=0).T
            return carry

        lax.fori_loop(0, REACH // 4, step, 0)
    near_items(items, rows_of, table, wanted, out, kept, highs, lows, total[0])


def couple(t_nodes, s_nodes, expansions):
    tiles = []
    for s in s_nodes:
        d = [t_nodes[q] - s[q : q + 1] for q in range(3)]
        tiles.append(lax.rsqrt(1.0 + (d[0] * d[0] + d[1] * d[1] + d[2] * d[2])))
    high, low = split(jnp.concatenate(tiles, axis=1))
    r = dot(jnp.concatenate([high, low], axis=0), expansions)
    return r[:K, :R] + r[:K, R:] + r[K:, :R]


def downward(
    boxes, coarse, n_dev, n_grp, far_one, far_two, counts, parents, uppers, where_am, *refs
):
    sent = refs[:n_dev]
    tops = refs[n_dev : n_dev + n_grp]
    basis, transfer, lower, own_nodes, two_rows, two_cols, near, out = refs[n_dev + n_grp : n_dev + n_grp + 8]
    m_one, m_two, n_one, l_two, g_left, g_right = refs[n_dev + n_grp + 8 :]
    dev, grp, box_base, coarse_base, group_base = [where_am[q] for q in range(5)]
    for k in range(n_dev):
        at = lax.rem(dev - k + n_dev, n_dev)
        data = sent[k]
        for b in range(boxes):
            m_one[at * boxes + b] = jnp.concatenate(split(data[:K, b * R : (b + 1) * R]), axis=1)
            n_one[at * boxes + b] = data[K : K + 8, b * K : (b + 1) * K] * 4.0
    for k in range(n_grp):
        at = lax.rem(grp - k + n_grp, n_grp)
        data = tops[k]
        for b in range(coarse):
            m_two[at * coarse + b] = jnp.concatenate(split(data[:, b * R : (b + 1) * R]), axis=1)

    def level_two(t, carry):
        a = coarse_base + t
        index = [far_two[a, q] for q in range(far_two.shape[1])]
        start = pl.ds(pl.multiple_of(a * K, K), K)
        t_nodes = [two_cols[start, q : q + 1] * 4.0 for q in range(3)]
        s_nodes = [
            jnp.concatenate([two_rows[index[q]], two_rows[index[q + 1]]], axis=1) * 4.0
            for q in range(0, len(index), 2)
        ]
        l_two[t] = couple(t_nodes, s_nodes, jnp.concatenate([m_two[q] for q in index], axis=0))
        return carry

    lax.fori_loop(0, coarse, level_two, 0)

    zero = jnp.zeros((K, R), BF16)

    def level_one(t, carry):
        index = [far_one[t, q] - group_base for q in range(far_one.shape[1])]
        start = pl.ds(pl.multiple_of(t * K, K), K)
        t_nodes = [own_nodes[start, q : q + 1] * 4.0 for q in range(3)]
        s_nodes = [
            jnp.concatenate([n_one[index[q]], n_one[index[q + 1]]], axis=1) for q in range(0, len(index), 2)
        ]
        g = couple(t_nodes, s_nodes, jnp.concatenate([m_one[q] for q in index], axis=0))
        chosen = l_two[uppers[t] - coarse_base]
        g = g + jnp.dot(lower[t], chosen, precision=HIGH, preferred_element_type=F32)
        high, low = split(g)
        g_left[t] = jnp.concatenate([high, zero, low, zero], axis=1)
        g_right[t] = jnp.concatenate([zero, high, zero, low], axis=1)
        return carry

    lax.fori_loop(0, boxes, level_one, 0)

    def pair(at):
        e_two = jnp.concatenate(split(transfer[:, pl.ds(pl.multiple_of(at * 2 * K, 2 * K), 2 * K)]), axis=0)
        p_zero = parents[at * 2] - box_base
        p_one = parents[at * 2 + 1] - box_base
        r = dot(e_two, jnp.concatenate([g_left[p_zero], g_right[p_one]], axis=0))
        g = r[:K, : 2 * R] + r[:K, 2 * R :] + r[K:, : 2 * R]
        turned = jnp.concatenate([g, g], axis=0).T
        high, low = split(turned)
        for side in range(2):
            c = at * 2 + side
            where = pl.ds(pl.multiple_of(c * B, B), B)
            b_two = jnp.concatenate(split(basis[:, where]), axis=0)
            rows = slice(side * R, (side + 1) * R)
            f = dot(jnp.concatenate([high[rows], low[rows]], axis=0), b_two)
            out[:, where] = masked(near[c] + (f[:R] + f[R:]), counts[c])

    group = 4

    def step(i, carry):
        for q in range(group):
            pair(i * group + q)
        return carry

    lax.fori_loop(0, near.shape[0] // 2 // group, step, 0)


def lists(slots, taken, counts):
    leaves = slots.shape[0]
    known = jnp.arange(counts.shape[0], dtype=jnp.int32)
    own = jnp.sum(jnp.where(slots[:, :, None] == known, counts, 0), axis=-1)
    blocks = jnp.where(taken, (own + ROWS - 1) // ROWS, 0)
    ends = jnp.sum(
        jnp.where(jnp.arange(NEAR)[:, None] >= jnp.arange(NEAR)[None, :], blocks[:, None, :], 0), axis=-1
    )
    starts = ends - blocks
    place = jnp.arange(SPAN, dtype=jnp.int32)
    inside = (place >= starts[:, :, None]) & (place < ends[:, :, None])
    null = counts.shape[0] * B
    base = (slots * B - starts * ROWS - null)[:, :, None]
    rows_of = null + jnp.sum(jnp.where(inside, base + place * ROWS, 0), axis=1)
    chunks = (ends[:, -1] + PER - 1) // PER
    leaf = jnp.arange(leaves, dtype=jnp.int32)
    after = jnp.sum(jnp.where(leaf[:, None] >= leaf[None, :], chunks[None, :], 0), axis=1)
    total = after[-1]
    t = jnp.arange(leaves * NEAR + UNROLL, dtype=jnp.int32)
    passed = t[:, None] >= after[None, :]
    at_leaf = jnp.sum(passed.astype(jnp.int32), axis=1)
    at_chunk = t - jnp.sum(jnp.where(passed, chunks[None, :], 0), axis=1)
    items = jnp.where(t < total, at_leaf * 16 + at_chunk, (leaves - 1) * 16 + NEAR)
    return items, rows_of, total.reshape(1)


def shifted(x, axis, by):
    count = lax.axis_size(axis)
    return lax.ppermute(x, axis, [(i, (i + by) % count) for i in range(count)])


def local(
    points,
    rhs,
    leaf_count,
    near_list,
    leaf_basis,
    leaf_transfer,
    leaf_parent,
    nodes1,
    box_transfer,
    box_parent,
    far1,
    nodes2,
    far2,
):
    leaves = leaf_count.shape[0]
    n_dev = lax.axis_size("dev")
    n_grp = lax.axis_size("grp")
    grp = lax.axis_index("grp")
    dev = lax.axis_index("dev")
    device = grp * n_dev + dev
    boxes = nodes1.shape[1] // K
    coarse = boxes * n_dev // CHILD
    width = REACH * B
    shape = jax.ShapeDtypeStruct

    up = [(i, i + 1) for i in range(n_dev - 1)]
    down = [(i + 1, i) for i in range(n_dev - 1)]
    both = jnp.concatenate([rhs, points], axis=0)
    before = lax.ppermute(both[:, -width:], "dev", up)
    after = lax.ppermute(both[:, :width], "dev", down)
    count_before = lax.ppermute(leaf_count[-REACH:], "dev", up)
    count_after = lax.ppermute(leaf_count[:REACH], "dev", down)
    halo_counts = jnp.concatenate([count_before, count_after])

    offset = jnp.stack([device * boxes, grp * coarse]).astype(jnp.int32)
    table, wanted, sent = pl.pallas_call(
        lambda *refs: upward(boxes, coarse, None, *refs),
        in_specs=[vmem()] * 6 + [smem()] * 4,
        out_specs=[vmem()] * 3,
        out_shape=[
            shape((leaves * B + ROWS, 2 * K), BF16),
            shape((leaves, K, B), BF16),
            shape((K + 8, (boxes + coarse) * R), F32),
        ],
        scratch_shapes=[
            pltpu.VMEM((boxes, R, 2 * K), F32),
            pltpu.VMEM((boxes, R, 2 * K), F32),
            pltpu.VMEM((coarse, R, K), F32),
        ],
        compiler_params=params(),
        name="upward",
    )(points, rhs, leaf_basis, leaf_transfer, nodes1, box_transfer, leaf_count, leaf_parent, box_parent, offset)

    all_sent = [sent] + [shifted(sent, "dev", k) for k in range(1, n_dev)]

    relative = near_list - device * leaves
    inside = (relative >= 0) & (relative < leaves)
    own_lists = lists(relative, inside, leaf_count)
    halo_slot = jnp.where(relative < 0, relative + REACH, relative - leaves + REACH)
    halo_lists = lists(halo_slot, ~inside, halo_counts)

    buffers = [pltpu.VMEM((B, 2 * K), BF16)] * UNROLL + [pltpu.VMEM((B, B), BF16)] * (2 * UNROLL)
    near = pl.pallas_call(
        near_own,
        in_specs=[smem()] * 3 + [vmem()] * 2,
        out_specs=vmem(),
        out_shape=shape((leaves, R, B), F32),
        scratch_shapes=buffers,
        compiler_params=params(),
        name="near_own",
    )(*own_lists, table, wanted)

    part = all_sent[0][:K, boxes * R :]
    for other in all_sent[1:]:
        part = part + other[:K, boxes * R :]
    tops = [part] + [shifted(part, "grp", k) for k in range(1, n_grp)]

    near = pl.pallas_call(
        near_halo,
        in_specs=[smem()] * 4 + [vmem()] * 4,
        out_specs=vmem(),
        out_shape=shape((leaves, R, B), F32),
        scratch_shapes=[pltpu.VMEM((2 * REACH * B + ROWS, 2 * K), BF16)] + buffers,
        compiler_params=params(),
        name="near_halo",
    )(*halo_lists, halo_counts, before, after, wanted, near)

    total_coarse = nodes2.shape[1] // K
    two_rows = jnp.pad(nodes2.reshape(3, total_coarse, K).transpose(1, 0, 2), ((0, 0), (0, 5), (0, 0)))
    where_am = jnp.stack([dev, grp, device * boxes, grp * coarse, grp * boxes * n_dev]).astype(jnp.int32)
    return pl.pallas_call(
        lambda *refs: downward(boxes, coarse, n_dev, n_grp, *refs),
        in_specs=[smem()] * 6 + [vmem()] * (n_dev + n_grp + 7),
        out_specs=vmem(),
        out_shape=shape((R, leaves * B), F32),
        scratch_shapes=[
            pltpu.VMEM((boxes * n_dev, K, 2 * R), BF16),
            pltpu.VMEM((total_coarse, K, 2 * R), BF16),
            pltpu.VMEM((boxes * n_dev, 8, K), F32),
            pltpu.VMEM((coarse, K, R), F32),
            pltpu.VMEM((boxes, K, 4 * R), BF16),
            pltpu.VMEM((boxes, K, 4 * R), BF16),
        ],
        compiler_params=params(),
        name="downward",
    )(
        far1,
        far2,
        leaf_count,
        leaf_parent,
        box_parent,
        where_am,
        *all_sent,
        *tops,
        leaf_basis,
        leaf_transfer,
        box_transfer.reshape(K, boxes, K).transpose(1, 0, 2),
        nodes1.T,
        two_rows,
        nodes2.T,
        near,
    )


def solution(mesh):
    placed = (
        P(None, ("grp", "dev")),
        P(None, ("grp", "dev")),
        P(("grp", "dev")),
        P(("grp", "dev"), None),
        P(None, ("grp", "dev")),
        P(None, ("grp", "dev")),
        P(("grp", "dev")),
        P(None, ("grp", "dev")),
        P(None, ("grp", "dev")),
        P(("grp", "dev")),
        P(("grp", "dev"), None),
        P(),
        P(),
    )
    return jax.shard_map(
        local, mesh=mesh, in_specs=placed, out_specs=P(None, ("grp", "dev")), check_vma=False
    )
```

profile of v0, /device:TPU:4, one launch (start us, length us, event | category | flops | bytes accessed | tf_op | source)
XLA Modules:
  0.0 157.4 jit_solution(7408290018666537953)
XLA Ops:
  0.7 16.6 %upward.1 = (bf16[16400,128]{1,0:T(8,128)(2,1)}, bf16[64,64,256]{2,1,0:T(8,128)(2,1)}, f32[72,512]{1,0:T(8,128)}) custom-call(f32[3,16384]{1,0:T(4,128)} %refs_0_.2, f32[32,16384]{1,0:T(8,128)} %refs_1_.2, f32[64,16384]{1,0:T(8,128)} %refs_18_.1, f32[64,4096]{1,0:T(8,128)} %refs_19_.1, f32[3,512]{1,0:T(4,128)} %refs_4_.2, f32[64,512]{1,0:T(8,128)} %refs_5_.1, ...), custom_call_target="tpu_custom_call" | custom-call | tf_op jit(solution)/shard_map/upward/pallas_call | solution.py:384
  17.2 1.5 collective-permute-start.1
  18.8 1.4 collective-permute-start.2
  20.2 1.9 %collective-permute-start.10 = (s32[32]{0:T(128)S(1)}, s32[32]{0:T(128)S(1)}, u32[]{:S(2)}, u32[]{:S(2)}) collective-permute-start(s32[32]{0:T(128)S(1)} %get-tuple-element.31), channel_id=1, source_target_pairs={{0,1},{1,2},{2,3},{3,4},{4,5},{5,6},{6,7},{8,9},{9,10},{10,11},{11... | collective-permute-start | bytes 392 | tf_op jit(solution)/shard_map/ppermute | solution.py:379
  22.1 4.5 %collective-permute-start.11 = (s32[32]{0:T(128)S(1)}, s32[32]{0:T(128)S(1)}, u32[]{:S(2)}, u32[]{:S(2)}) collective-permute-start(s32[32]{0:T(128)S(1)} %get-tuple-element.32), channel_id=1, source_target_pairs={{1,0},{2,1},{3,2},{4,3},{5,4},{6,5},{7,6},{9,8},{10,9},{11,10},{12... | collective-permute-start | bytes 392 | tf_op jit(solution)/shard_map/ppermute | solution.py:380
  28.6 1.3 copy.57
  30.2 1.2 select_reduce_fusion.2
  31.6 1.8 %fusion.8 = (f32[35,8192]{1,0:T(8,128)}, f32[35,8192]{1,0:T(8,128)}) fusion(f32[35,16384]{1,0:T(8,128)S(1)} %constant_dynamic-update-slice_fusion), kind=kLoop, calls=%fused_computation.75 | loop fusion | bytes 4587520 | tf_op jit(solution)/shard_map/slice | solution.py:378
  36.2 1.9 %collective-permute-start.12 = (f32[35,8192]{1,0:T(8,128)}, f32[35,8192]{1,0:T(8,128)S(1)}, u32[]{:S(2)}, u32[]{:S(2)}) collective-permute-start(f32[35,8192]{1,0:T(8,128)} %get-tuple-element.28), channel_id=1, source_target_pairs={{0,1},{1,2},{2,3},{3,4},{4,5},{5,6},{6,7},{8,9},{9,10},{10,11},{11... | collective-permute-start | bytes 3440648 | tf_op jit(solution)/shard_map/ppermute | solution.py:377
  38.2 4.5 %collective-permute-start.13 = (f32[35,8192]{1,0:T(8,128)}, f32[35,8192]{1,0:T(8,128)S(1)}, u32[]{:S(2)}, u32[]{:S(2)}) collective-permute-start(f32[35,8192]{1,0:T(8,128)} %get-tuple-element.27), channel_id=1, source_target_pairs={{1,0},{2,1},{3,2},{4,3},{5,4},{6,5},{7,6},{9,8},{10,9},{11,10},{12... | collective-permute-start | bytes 3440648 | tf_op jit(solution)/shard_map/ppermute | solution.py:378
  42.8 1.2 select_reduce_fusion.3
  47.5 1.2 add_select_fusion.2.items
  48.7 1.7 %collective-permute-start.5 = (f32[72,512]{1,0:T(8,128)S(1)}, f32[72,512]{1,0:T(8,128)S(1)}, u32[]{:S(2)}, u32[]{:S(2)}) collective-permute-start(f32[72,512]{1,0:T(8,128)S(1)} %copy-done.5), channel_id=1, source_target_pairs={{0,6},{1,7},{2,0},{3,1},{4,2},{5,3},{6,4},{7,5},{8,14},{9,15},{10,... | collective-permute-start | bytes 442376 | tf_op jit(solution)/shard_map/ppermute | solution.py:345
  50.4 4.1 %collective-permute-done.3.refs_10_ = f32[72,512]{1,0:T(8,128)S(1)} collective-permute-done((f32[72,512]{1,0:T(8,128)S(1)}, f32[72,512]{1,0:T(8,128)S(1)}, u32[]{:S(2)}, u32[]{:S(2)}) %collective-permute-start.3) | collective-permute-done | bytes 147488 | tf_op jit(solution)/shard_map/ppermute | solution.py:345
  54.5 2.0 %collective-permute-start.6 = (f32[72,512]{1,0:T(8,128)S(1)}, f32[72,512]{1,0:T(8,128)S(1)}, u32[]{:S(2)}, u32[]{:S(2)}) collective-permute-start(f32[72,512]{1,0:T(8,128)S(1)} %copy-done.5), channel_id=1, source_target_pairs={{0,7},{1,0},{2,1},{3,2},{4,3},{5,4},{6,5},{7,6},{8,15},{9,8},{10,9... | collective-permute-start | bytes 442376 | tf_op jit(solution)/shard_map/ppermute | solution.py:345
  57.4 14.9 %collective-permute-done.5.refs_12_ = f32[72,512]{1,0:T(8,128)S(1)} collective-permute-done((f32[72,512]{1,0:T(8,128)S(1)}, f32[72,512]{1,0:T(8,128)S(1)}, u32[]{:S(2)}, u32[]{:S(2)}) %collective-permute-start.5) | collective-permute-done | bytes 147488 | tf_op jit(solution)/shard_map/ppermute | solution.py:345
  72.3 1.6 %collective-permute-done.6.refs_13_ = f32[72,512]{1,0:T(8,128)S(1)} collective-permute-done((f32[72,512]{1,0:T(8,128)S(1)}, f32[72,512]{1,0:T(8,128)S(1)}, u32[]{:S(2)}, u32[]{:S(2)}) %collective-permute-start.6) | collective-permute-done | bytes 147488 | tf_op jit(solution)/shard_map/ppermute | solution.py:345
  74.8 1.6 %collective-permute-start.7 = (f32[64,256]{1,0:T(8,128)S(1)}, f32[64,256]{1,0:T(8,128)S(1)}, u32[]{:S(2)}, u32[]{:S(2)}) collective-permute-start(f32[64,256]{1,0:T(8,128)S(1)} %slice_add_fusion.refs_14_), channel_id=1, source_target_pairs={{0,8},{8,16},{16,24},{24,0},{1,9},{9,17},{17,25},{25,1},{2,10},{10... | collective-permute-start | bytes 196616 | tf_op jit(solution)/shard_map/ppermute | solution.py:345
  76.5 2.6 %collective-permute-start.8 = (f32[64,256]{1,0:T(8,128)S(1)}, f32[64,256]{1,0:T(8,128)S(1)}, u32[]{:S(2)}, u32[]{:S(2)}) collective-permute-start(f32[64,256]{1,0:T(8,128)S(1)} %slice_add_fusion.refs_14_), channel_id=1, source_target_pairs={{0,16},{8,24},{16,0},{24,8},{1,17},{9,25},{17,1},{25,9},{2,18},{10... | collective-permute-start | bytes 196616 | tf_op jit(solution)/shard_map/ppermute | solution.py:345
  79.0 1.3 collective-permute-start.9
  80.4 1.2 add_select_fusion.3.items
  81.6 33.8 %near_own.1.begun = f32[64,32,256]{2,1,0:T(8,128)} custom-call(s32[520]{0:T(1024)} %add_select_fusion.2.items, s32[64,144]{1,0:T(8,128)} %broadcast_add_fusion.rows_of, s32[1]{0:T(128)} %slice.63.total, bf16[16400,128]{1,0:T(8,128)(2,1)} %get-tuple-element.10.table, bf16[64,64,256]{2,1,0:T(8,128)(2,1)} %get-tuple-element.9.wanted), custom_call_target="tpu_custom_call" | custom-call | tf_op jit(solution)/shard_map/near_own/pallas_call | solution.py:411
  117.6 16.4 %near_halo.1.refs_24_ = f32[64,32,256]{2,1,0:T(8,128)} custom-call(s32[520]{0:T(1024)} %add_select_fusion.3.items, s32[64,144]{1,0:T(8,128)} %broadcast_add_fusion.1.rows_of, s32[1]{0:T(128)} %slice.59.total, s32[64]{0:T(128)} %copy-done.20, f32[35,8192]{1,0:T(8,128)} %copy-done.1, f32[35,8192]{1,0:T(8,128)} %copy-done.2, ...), custom_call_target="tpu_custom_call" | custom-call | tf_op jit(solution)/shard_map/near_halo/pallas_call | solution.py:426
  134.7 22.7 %downward.1 = f32[32,16384]{1,0:T(8,128)} custom-call(s32[8,16]{1,0:T(8,128)} %refs_0_.3, s32[32,8]{1,0:T(8,128)} %copy.68.refs_1_, s32[64]{0:T(128)} %refs_2_.3, s32[64]{0:T(128)} %refs_3_.3, s32[8]{0:T(128)} %refs_4_.3, s32[5]{0:T(128)} %stack.28.refs_5_, f32[72,512]{1,0:T(8,128)} %get-tuple-element.8.refs_6_, f32[72,512]{1,0:T(8,128)} %copy-done.6, ...), custom_call_target="tpu_custom_call" | custom-call | tf_op jit(solution)/shard_map/downward/pallas_call | solution.py:439
  (97 shorter events, 14.0 us)
Async XLA Ops:
  0.7 19.5 %copy-start.17 = (s32[64]{0:T(128)S(1)}, s32[64]{0:T(128)}, u32[]{:S(2)}) copy-start(s32[64]{0:T(128)} %refs_2_.3) | copy-start | bytes 772
  0.7 26.0 %copy-start = (f32[32,16384]{1,0:T(8,128)S(1)}, f32[32,16384]{1,0:T(8,128)}, u32[]{:S(2)}) copy-start(f32[32,16384]{1,0:T(8,128)} %refs_1_.2) | copy-start | bytes 6291460
  17.2 30.2 %collective-permute-start = (f32[72,512]{1,0:T(8,128)}, f32[72,512]{1,0:T(8,128)S(1)}, u32[]{:S(2)}, u32[]{:S(2)}) collective-permute-start(f32[72,512]{1,0:T(8,128)} %get-tuple-element.8.refs_6_), channel_id=1, source_target_pairs={{0,1},{1,2},{2,3},{3,4},{4,5},{5,6},{6,7},{7,0},{8,9},{9,10},{10,1... | collective-permute-start | bytes 442376 | tf_op jit(solution)/shard_map/ppermute | solution.py:345
  17.2 31.5 %collective-permute-start.1 = (f32[72,512]{1,0:T(8,128)}, f32[72,512]{1,0:T(8,128)}, u32[]{:S(2)}, u32[]{:S(2)}) collective-permute-start(f32[72,512]{1,0:T(8,128)} %get-tuple-element.8.refs_6_), channel_id=1, source_target_pairs={{0,2},{1,3},{2,4},{3,5},{4,6},{5,7},{6,0},{7,1},{8,10},{9,11},{10,... | collective-permute-start | bytes 442376 | tf_op jit(solution)/shard_map/ppermute | solution.py:345
  18.8 29.9 %collective-permute-start.2 = (f32[72,512]{1,0:T(8,128)}, f32[72,512]{1,0:T(8,128)}, u32[]{:S(2)}, u32[]{:S(2)}) collective-permute-start(f32[72,512]{1,0:T(8,128)} %get-tuple-element.8.refs_6_), channel_id=1, source_target_pairs={{0,3},{1,4},{2,5},{3,6},{4,7},{5,0},{6,1},{7,2},{8,11},{9,12},{10,... | collective-permute-start | bytes 442376 | tf_op jit(solution)/shard_map/ppermute | solution.py:345
  20.2 16.0 %collective-permute-start.10 = (s32[32]{0:T(128)S(1)}, s32[32]{0:T(128)S(1)}, u32[]{:S(2)}, u32[]{:S(2)}) collective-permute-start(s32[32]{0:T(128)S(1)} %get-tuple-element.31), channel_id=1, source_target_pairs={{0,1},{1,2},{2,3},{3,4},{4,5},{5,6},{6,7},{8,9},{9,10},{10,11},{11... | collective-permute-start | bytes 392 | tf_op jit(solution)/shard_map/ppermute | solution.py:379
  22.1 16.0 %collective-permute-start.11 = (s32[32]{0:T(128)S(1)}, s32[32]{0:T(128)S(1)}, u32[]{:S(2)}, u32[]{:S(2)}) collective-permute-start(s32[32]{0:T(128)S(1)} %get-tuple-element.32), channel_id=1, source_target_pairs={{1,0},{2,1},{3,2},{4,3},{5,4},{6,5},{7,6},{9,8},{10,9},{11,10},{12... | collective-permute-start | bytes 392 | tf_op jit(solution)/shard_map/ppermute | solution.py:380
  31.6 15.8 %copy-start.5 = (f32[72,512]{1,0:T(8,128)S(1)}, f32[72,512]{1,0:T(8,128)}, u32[]{:S(2)}) copy-start(f32[72,512]{1,0:T(8,128)} %get-tuple-element.8.refs_6_) | copy-start | bytes 442372
  36.2 79.2 %collective-permute-start.12 = (f32[35,8192]{1,0:T(8,128)}, f32[35,8192]{1,0:T(8,128)S(1)}, u32[]{:S(2)}, u32[]{:S(2)}) collective-permute-start(f32[35,8192]{1,0:T(8,128)} %get-tuple-element.28), channel_id=1, source_target_pairs={{0,1},{1,2},{2,3},{3,4},{4,5},{5,6},{6,7},{8,9},{9,10},{10,11},{11... | collective-permute-start | bytes 3440648 | tf_op jit(solution)/shard_map/ppermute | solution.py:377
  38.2 77.3 %collective-permute-start.13 = (f32[35,8192]{1,0:T(8,128)}, f32[35,8192]{1,0:T(8,128)S(1)}, u32[]{:S(2)}, u32[]{:S(2)}) collective-permute-start(f32[35,8192]{1,0:T(8,128)} %get-tuple-element.27), channel_id=1, source_target_pairs={{1,0},{2,1},{3,2},{4,3},{5,4},{6,5},{7,6},{9,8},{10,9},{11,10},{12... | collective-permute-start | bytes 3440648 | tf_op jit(solution)/shard_map/ppermute | solution.py:378
  42.8 72.6 %copy-start.20 = (s32[64]{0:T(128)}, s32[64]{0:T(128)S(1)}, u32[]{:S(2)}) copy-start(s32[64]{0:T(128)S(1)} %pad_add_fusion.1.counts) | copy-start | bytes 772
  47.4 67.9 %copy-start.6 = (f32[72,512]{1,0:T(8,128)}, f32[72,512]{1,0:T(8,128)S(1)}, u32[]{:S(2)}) copy-start(f32[72,512]{1,0:T(8,128)S(1)} %collective-permute-done.refs_7_) | copy-start | bytes 442372
  47.5 7.1 %collective-permute-start.3 = (f32[72,512]{1,0:T(8,128)S(1)}, f32[72,512]{1,0:T(8,128)S(1)}, u32[]{:S(2)}, u32[]{:S(2)}) collective-permute-start(f32[72,512]{1,0:T(8,128)S(1)} %copy-done.5), channel_id=1, source_target_pairs={{0,4},{1,5},{2,6},{3,7},{4,0},{5,1},{6,2},{7,3},{8,12},{9,13},{10,... | collective-permute-start | bytes 442376 | tf_op jit(solution)/shard_map/ppermute | solution.py:345
  48.7 8.7 %collective-permute-start.4 = (f32[72,512]{1,0:T(8,128)S(1)}, f32[72,512]{1,0:T(8,128)S(1)}, u32[]{:S(2)}, u32[]{:S(2)}) collective-permute-start(f32[72,512]{1,0:T(8,128)S(1)} %copy-done.5), channel_id=1, source_target_pairs={{0,5},{1,6},{2,7},{3,0},{4,1},{5,2},{6,3},{7,4},{8,13},{9,14},{10,... | collective-permute-start | bytes 442376 | tf_op jit(solution)/shard_map/ppermute | solution.py:345
  48.7 23.6 %collective-permute-start.5 = (f32[72,512]{1,0:T(8,128)S(1)}, f32[72,512]{1,0:T(8,128)S(1)}, u32[]{:S(2)}, u32[]{:S(2)}) collective-permute-start(f32[72,512]{1,0:T(8,128)S(1)} %copy-done.5), channel_id=1, source_target_pairs={{0,6},{1,7},{2,0},{3,1},{4,2},{5,3},{6,4},{7,5},{8,14},{9,15},{10,... | collective-permute-start | bytes 442376 | tf_op jit(solution)/shard_map/ppermute | solution.py:345
  54.5 60.9 %copy-start.7 = (f32[72,512]{1,0:T(8,128)}, f32[72,512]{1,0:T(8,128)S(1)}, u32[]{:S(2)}) copy-start(f32[72,512]{1,0:T(8,128)S(1)} %collective-permute-done.3.refs_10_) | copy-start | bytes 442372
  54.5 19.3 %collective-permute-start.6 = (f32[72,512]{1,0:T(8,128)S(1)}, f32[72,512]{1,0:T(8,128)S(1)}, u32[]{:S(2)}, u32[]{:S(2)}) collective-permute-start(f32[72,512]{1,0:T(8,128)S(1)} %copy-done.5), channel_id=1, source_target_pairs={{0,7},{1,0},{2,1},{3,2},{4,3},{5,4},{6,5},{7,6},{8,15},{9,8},{10,9... | collective-permute-start | bytes 442376 | tf_op jit(solution)/shard_map/ppermute | solution.py:345
  57.4 58.0 %copy-start.8 = (f32[72,512]{1,0:T(8,128)}, f32[72,512]{1,0:T(8,128)S(1)}, u32[]{:S(2)}) copy-start(f32[72,512]{1,0:T(8,128)S(1)} %collective-permute-done.4.refs_11_) | copy-start | bytes 442372
  72.3 43.1 %copy-start.9 = (f32[72,512]{1,0:T(8,128)}, f32[72,512]{1,0:T(8,128)S(1)}, u32[]{:S(2)}) copy-start(f32[72,512]{1,0:T(8,128)S(1)} %collective-permute-done.5.refs_12_) | copy-start | bytes 442372
  73.8 41.6 %copy-start.10 = (f32[72,512]{1,0:T(8,128)}, f32[72,512]{1,0:T(8,128)S(1)}, u32[]{:S(2)}) copy-start(f32[72,512]{1,0:T(8,128)S(1)} %collective-permute-done.6.refs_13_) | copy-start | bytes 442372
  74.8 40.6 %copy-start.11 = (f32[64,256]{1,0:T(8,128)}, f32[64,256]{1,0:T(8,128)S(1)}, u32[]{:S(2)}) copy-start(f32[64,256]{1,0:T(8,128)S(1)} %slice_add_fusion.refs_14_) | copy-start | bytes 196612
  74.8 59.2 %collective-permute-start.7 = (f32[64,256]{1,0:T(8,128)S(1)}, f32[64,256]{1,0:T(8,128)S(1)}, u32[]{:S(2)}, u32[]{:S(2)}) collective-permute-start(f32[64,256]{1,0:T(8,128)S(1)} %slice_add_fusion.refs_14_), channel_id=1, source_target_pairs={{0,8},{8,16},{16,24},{24,0},{1,9},{9,17},{17,25},{25,1},{2,10},{10... | collective-permute-start | bytes 196616 | tf_op jit(solution)/shard_map/ppermute | solution.py:345
  76.5 57.6 %collective-permute-start.8 = (f32[64,256]{1,0:T(8,128)S(1)}, f32[64,256]{1,0:T(8,128)S(1)}, u32[]{:S(2)}, u32[]{:S(2)}) collective-permute-start(f32[64,256]{1,0:T(8,128)S(1)} %slice_add_fusion.refs_14_), channel_id=1, source_target_pairs={{0,16},{8,24},{16,0},{24,8},{1,17},{9,25},{17,1},{25,9},{2,18},{10... | collective-permute-start | bytes 196616 | tf_op jit(solution)/shard_map/ppermute | solution.py:345
  79.0 55.0 %collective-permute-start.9 = (f32[64,256]{1,0:T(8,128)S(1)}, f32[64,256]{1,0:T(8,128)S(1)}, u32[]{:S(2)}, u32[]{:S(2)}) collective-permute-start(f32[64,256]{1,0:T(8,128)S(1)} %slice_add_fusion.refs_14_), channel_id=1, source_target_pairs={{0,24},{8,0},{16,8},{24,16},{1,25},{9,1},{17,9},{25,17},{2,26},{10... | collective-permute-start | bytes 196616 | tf_op jit(solution)/shard_map/ppermute | solution.py:345
  (11 other events, 18.5 us)
where the time goes:
time: 160 us; the launch traced here: 157 us
  Pallas kernels  89.5 us (56%)
  starting transfers between devices  25.2 us (16%)
  waiting for transfers between devices  20.5 us (13%)
  local copies, waits for them, and re-layouts  12.8 us (8%)
  other arithmetic  8.99 us (6%)
    pallas_call x1, Pallas kernels, local(): pl.pallas_call(near_own, in_specs=[smem()] * 3 + [vmem()] * 2, out_specs=...  33.8 us
    pallas_call x1, Pallas kernels, local(): pl.pallas_call(lambda *refs: downward(boxes, coarse, n_dev, n_grp, *refs)...  22.7 us
    ppermute x10, waiting for transfers between devices, shifted(): return lax.ppermute(x, axis, [(i, (i + by) % count) for i in range(count)])  20.5 us
    pallas_call x1, Pallas kernels, local(): pl.pallas_call(lambda *refs: upward(boxes, coarse, None, *refs), in_specs...  16.6 us
    pallas_call x1, Pallas kernels, local(): pl.pallas_call(near_halo, in_specs=[smem()] * 4 + [vmem()] * 4, out_specs...  16.4 us
    ppermute x10, starting transfers between devices, shifted(): return lax.ppermute(x, axis, [(i, (i + by) % count) for i in range(count)])  12.3 us
    unnamed x46, local copies, waits for them, and re-layouts  6.54 us
    ppermute x1, starting transfers between devices, local(): count_after = lax.ppermute(leaf_count[:REACH], 'dev', down)  4.54 us
  transfers between devices with their start and end apart: 14, of which 3 were waited for; matrix products, arithmetic and copies ran while one was open for 11% of the time, Pallas kernels for 32%

commit v1 on v0

v1 whole, which is shorter than its diff:
```python
import jax
import jax.numpy as jnp
from jax import lax
from jax.experimental import pallas as pl
from jax.experimental.pallas import tpu as pltpu
from jax.sharding import PartitionSpec as P

B = 256
K = 64
R = 32
NEAR = 8
CHILD = 8
REACH = 32
ROWS = 16
PER = B // ROWS
UNROLL = 8
SPAN = NEAR * PER + PER

F32 = jnp.float32
BF16 = jnp.bfloat16
LIMIT = 58 * 1024 * 1024

PIECES = ((0, 0), (0, 1), (1, 0), (1, 1), (0, 2), (2, 0), (1, 2), (2, 1))


def params():
    return pltpu.CompilerParams(vmem_limit_bytes=LIMIT)


def cost(us):
    return pl.CostEstimate(flops=us * 10**9, bytes_accessed=us * 3 * 10**6, transcendentals=0)


def vmem():
    return pl.BlockSpec(memory_space=pltpu.VMEM)


def smem():
    return pl.BlockSpec(memory_space=pltpu.SMEM)


def split(x):
    high = x.astype(BF16)
    return high, (x - high.astype(F32)).astype(BF16)


def to_grid(x, step):
    big = 1.5 * 2.0**23 * step
    return (x + big) - big


def dot(a, b):
    return jnp.dot(a, b, preferred_element_type=F32)


def dot_nt(a, b):
    return lax.dot_general(a, b, (((1,), (1,)), ((), ())), preferred_element_type=F32)


def features(coords, targets=True):
    n = coords.shape[1]
    scaled = jnp.concatenate([coords * 4.0, jnp.zeros((5, n), F32)], axis=0)
    one = to_grid(scaled, 2.0**-3)
    rest = scaled - one
    two = to_grid(rest, 2.0**-11)
    three = rest - two
    pieces = (one, two, three)
    square = jnp.sum(one * one, axis=0, keepdims=True)
    s_one = to_grid(square, 8.0)
    s_two = square - s_one
    tail = jnp.sum(rest * (scaled + one), axis=0, keepdims=True)
    q_one = to_grid(tail, 2.0**-4)
    tail = tail - q_one
    q_two = to_grid(tail, 2.0**-12)
    norms = (s_one, s_two, q_one, q_two, tail - q_two)
    row = lax.broadcasted_iota(jnp.int32, (8, n), 0)
    sources, wanted = [], []
    for at, (first, second) in enumerate(PIECES):
        src = pieces[first]
        tgt = pieces[second] * -2.0
        if at < 5:
            src = jnp.where(row == 3, norms[at], jnp.where(row == 4, 1.0, src))
            tgt = jnp.where(row == 3, 1.0, jnp.where(row == 4, norms[at], tgt))
        elif at == 5:
            src = jnp.where(row == 3, 1.0, src)
            tgt = jnp.where(row == 3, 1.0, tgt)
        sources.append(src)
        wanted.append(tgt)
    source = jnp.concatenate(sources, axis=0).astype(BF16)
    if not targets:
        return source, None
    return source, jnp.concatenate(wanted, axis=0).astype(BF16)


def masked(x, count):
    slot = lax.broadcasted_iota(jnp.int32, x.shape, 1)
    return jnp.where(slot < count, x, 0.0)


def lists(slots, taken, counts, null):
    leaves = slots.shape[0]
    lane = lax.broadcasted_iota(jnp.int32, (leaves, counts.shape[1]), 1)
    place = lax.broadcasted_iota(jnp.int32, (leaves, SPAN), 1)
    rows_of = jnp.full((leaves, SPAN), null, jnp.int32)
    start = jnp.zeros((leaves, 1), jnp.int32)
    for e in range(NEAR):
        slot = slots[:, e : e + 1]
        count = jnp.sum(jnp.where(slot == lane, counts, 0.0), axis=1, keepdims=True).astype(jnp.int32)
        end = start + jnp.where(taken[:, e : e + 1], (count + ROWS - 1) // ROWS, 0)
        rows_of = jnp.where((place >= start) & (place < end), slot * B + (place - start) * ROWS, rows_of)
        start = end
    chunks = ((start + PER - 1) // PER).astype(F32)
    below = lax.broadcasted_iota(jnp.int32, (leaves, leaves), 0) >= lax.broadcasted_iota(
        jnp.int32, (leaves, leaves), 1
    )
    after = dot(below.astype(F32).astype(BF16), jnp.broadcast_to(chunks, (leaves, 128)).astype(BF16))
    width = -(-(leaves * NEAR + UNROLL) // 128) * 128
    t = lax.broadcasted_iota(jnp.int32, (leaves, width), 1).astype(F32)
    passed = t >= after[:, :1]
    at_leaf = jnp.sum(jnp.where(passed, 1.0, 0.0), axis=0, keepdims=True)
    at_chunk = t[:1] - jnp.sum(jnp.where(passed, chunks, 0.0), axis=0, keepdims=True)
    total = jnp.broadcast_to(after[leaves - 1 :, :1], (1, width))
    items = jnp.where(t[:1] < total, at_leaf * 16.0 + at_chunk, (leaves - 1) * 16.0 + NEAR)
    row = lax.broadcasted_iota(jnp.int32, (8, width), 0)
    return jnp.where(row == 0, items, total).astype(jnp.int32), rows_of


def upward(boxes, coarse, leaves, points, rhs, basis, transfer, nodes, lower, near, row_counts, counts, parents, uppers, offset, table, wanted, sent, items, rows_of, left, right, top):
    at_step = pl.program_id(0)
    group = wanted.shape[0]

    @pl.when(at_step == 0)
    def _():
        left[...] = jnp.zeros_like(left)
        right[...] = jnp.zeros_like(right)
        top[...] = jnp.zeros_like(top)
        slots = near[...] - offset[2]
        items[...], rows_of[...] = lists(slots, (slots >= 0) & (slots < leaves), row_counts[...].astype(F32), leaves * B)

    def pair(at):
        rows = []
        first = at_step * group + at * 2
        for side in range(2):
            c = at * 2 + side
            where = slice(c * B, (c + 1) * B)
            x = masked(rhs[:, where], counts[first + side])
            x_two = jnp.concatenate(split(x), axis=0)
            source, target = features(points[:, where])
            wanted[c] = target
            table[where, :] = jnp.concatenate([source, x_two], axis=0).T
            b_two = jnp.concatenate(split(basis[:, where]), axis=0)
            r = dot_nt(x_two, b_two)
            rows.append(r[:R, :K] + r[:R, K:] + r[R:, :K])
        m = jnp.concatenate(rows, axis=0)
        high, low = split(m)
        left_side = jnp.concatenate(
            [jnp.concatenate([high, high], axis=1), jnp.concatenate([low, low], axis=1)], axis=0
        )
        e_two = jnp.concatenate(split(transfer[:, at * 2 * K : (at + 1) * 2 * K]), axis=0)
        lifted = dot(left_side, e_two)
        lifted = lifted[: 2 * R] + lifted[2 * R :]
        left[parents[first] - offset[0]] += lifted[:R]
        right[parents[first + 1] - offset[0]] += lifted[R:]

    @pl.when(at_step * group < leaves)
    def _():
        for at in range(group // 2):
            pair(at)

    @pl.when(at_step * group >= leaves)
    def _():
        source, _ = features(jnp.zeros((3, B), F32), False)
        rows = jnp.concatenate([source, jnp.zeros((2 * R, B), BF16)], axis=0).T
        table[:B, :] = rows
        m_one = [left[b][:, :K] + right[b][:, K:] for b in range(boxes)]
        for b in range(boxes):
            f = lower[:, (b // 2) * 2 * K : (b // 2 + 1) * 2 * K]
            f_two = jnp.concatenate(split(f), axis=0)
            high, low = split(m_one[b])
            raised = dot(
                jnp.concatenate(
                    [jnp.concatenate([high, high], axis=1), jnp.concatenate([low, low], axis=1)], axis=0
                ),
                f_two,
            )
            raised = raised[:R] + raised[R:]
            top[uppers[b] - offset[1]] += raised[:, (b % 2) * K : (b % 2 + 1) * K]
        sent[K : K + 8, :] = jnp.zeros((8, sent.shape[1]), F32)
        sent[K : K + 3, : boxes * K] = nodes[...]
        for q in range(boxes // 4):
            block = jnp.concatenate(m_one[4 * q : 4 * q + 4], axis=0)
            sent[:K, q * 4 * R : (q + 1) * 4 * R] = block.T
        for q in range(coarse // 4):
            block = jnp.concatenate([top[4 * q + z] for z in range(4)], axis=0)
            sent[:K, (boxes + 4 * q) * R : (boxes + 4 * q + 4) * R] = block.T


def near_items(items, rows_of, table, wanted, out, kept, highs, lows):
    def first(t, s):
        code = items[0, t]
        c = code // 16
        base = (code % 16) * PER
        rows = jnp.concatenate(
            [table[pl.ds(pl.multiple_of(rows_of[c, base + q], ROWS), ROWS), :] for q in range(PER)], axis=0
        )
        kept[s][...] = rows
        u = dot(rows[:, :K], wanted[c])
        high, low = split(lax.rsqrt(u))
        highs[s][...] = high
        lows[s][...] = low

    def second(t, s):
        c = items[0, t] // 16
        x = kept[s][...].T[K:]
        a = dot(x, highs[s][...])
        b = dot(x[:R], lows[s][...])
        out[c] += a[:R] + a[R:] + b

    groups = (items[1, 0] + UNROLL - 1) // UNROLL

    @pl.when(groups > 0)
    def _():
        for q in range(UNROLL):
            first(q, q)

        def step(g, carry):
            for q in range(UNROLL):
                second((g - 1) * UNROLL + q, q)
                first(g * UNROLL + q, q)
            return carry

        lax.fori_loop(1, groups, step, 0)
        for q in range(UNROLL):
            second((groups - 1) * UNROLL + q, q)


def near_own(items, rows_of, table, wanted, out, *scratch):
    kept, highs, lows = scratch[:UNROLL], scratch[UNROLL : 2 * UNROLL], scratch[2 * UNROLL :]
    out[...] = jnp.zeros_like(out)
    near_items(items, rows_of, table, wanted, out, kept, highs, lows)


def halo_table(leaves, before, after, near, offset, table, items, rows_of, counts):
    at_step = pl.program_id(0)
    group = before.shape[1] // B
    side = table.shape[0] // 2 // B
    steps = REACH // group
    lane = lax.broadcasted_iota(jnp.int32, counts.shape, 1)

    @pl.when(at_step == 0)
    def _():
        counts[...] = jnp.zeros_like(counts)

    @pl.when(at_step < steps)
    def _():
        for part, data in ((0, before), (1, after)):
            for q in range(group):
                where = slice(q * B, (q + 1) * B)
                count = data[R + 3 : R + 4, where]
                slot = lax.broadcasted_iota(jnp.int32, (R, B), 1).astype(F32)
                x = jnp.where(slot < count, data[:R, where], 0.0)
                source, _ = features(data[R : R + 3, where], False)
                to = slice((part * side + q) * B, (part * side + q + 1) * B)
                table[to, :] = jnp.concatenate([source, *split(x)], axis=0).T
                slot = (at_step * 2 + part) * group + q
                counts[...] = jnp.where(lane == slot, count[:, :1], counts[...])

    @pl.when(at_step == steps)
    def _():
        source, _ = features(jnp.zeros((3, B), F32), False)
        table[:B, :] = jnp.concatenate([source, jnp.zeros((2 * R, B), BF16)], axis=0).T
        relative = near[...] - offset[2]
        taken = (relative < 0) | (relative >= leaves)
        h = jnp.where(relative < 0, relative + REACH, relative - leaves)
        slots = (h // group * 2 + jnp.where(relative < 0, 0, 1)) * group + h % group
        items[...], rows_of[...] = lists(slots, taken, counts[:1, : 2 * REACH], 2 * REACH * B)


def near_halo(items, rows_of, table, wanted, begun, out, *scratch):
    kept, highs, lows = scratch[:UNROLL], scratch[UNROLL : 2 * UNROLL], scratch[2 * UNROLL :]
    out[...] = begun[...]
    near_items(items, rows_of, table, wanted, out, kept, highs, lows)


def couple(t_nodes, s_nodes, expansions):
    tiles = []
    for s in s_nodes:
        d = [t_nodes[q] - s[q : q + 1] for q in range(3)]
        tiles.append(lax.rsqrt(1.0 + (d[0] * d[0] + d[1] * d[1] + d[2] * d[2])))
    high, low = split(jnp.concatenate(tiles, axis=1))
    r = dot(jnp.concatenate([high, low], axis=0), expansions)
    return r[:K, :R] + r[:K, R:] + r[K:, :R]


def columns(nodes):
    padded = jnp.concatenate([nodes * 4.0, jnp.zeros((5, nodes.shape[1]), F32)], axis=0)
    return padded.T


def downward(boxes, coarse, n_dev, n_grp, far_one, far_two, counts, parents, uppers, where_am, *refs):
    sent = refs[:n_dev]
    tops = refs[n_dev : n_dev + n_grp]
    basis, transfer, lower, nodes_one, nodes_two, near, out = refs[n_dev + n_grp : n_dev + n_grp + 7]
    m_one, m_two, n_one, n_two, c_one, c_two, l_two, g_left, g_right = refs[n_dev + n_grp + 7 :]
    dev, grp, box_base, coarse_base, group_base = [where_am[q] for q in range(5)]

    @pl.when(pl.program_id(0) == 0)
    def _():
        for k in range(n_dev):
            at = lax.rem(dev - k + n_dev, n_dev)
            data = sent[k]
            for b in range(boxes):
                m_one[at * boxes + b] = jnp.concatenate(split(data[:K, b * R : (b + 1) * R]), axis=1)
                n_one[at * boxes + b] = data[K : K + 8, b * K : (b + 1) * K] * 4.0
        for k in range(n_grp):
            at = lax.rem(grp - k + n_grp, n_grp)
            data = tops[k]
            for b in range(coarse):
                m_two[at * coarse + b] = jnp.concatenate(split(data[:, b * R : (b + 1) * R]), axis=1)
        for b in range(n_grp * coarse):
            n_two[b, :3] = nodes_two[:, b * K : (b + 1) * K] * 4.0
        c_one[...] = columns(nodes_one[...])
        c_two[...] = columns(nodes_two[...])

        def tiles(nodes, index):
            return [
                jnp.concatenate([nodes[index[q]], nodes[index[q + 1]]], axis=1) for q in range(0, len(index), 2)
            ]

        for t in range(coarse):
            a = coarse_base + t
            index = [far_two[a, q] for q in range(far_two.shape[1])]
            start = pl.ds(pl.multiple_of(a * K, K), K)
            t_nodes = [c_two[start, q : q + 1] for q in range(3)]
            l_two[t] = couple(t_nodes, tiles(n_two, index), jnp.concatenate([m_two[q] for q in index], axis=0))

        zero = jnp.zeros((K, R), BF16)
        for t in range(boxes):
            index = [far_one[t, q] - group_base for q in range(far_one.shape[1])]
            t_nodes = [c_one[t * K : (t + 1) * K, q : q + 1] for q in range(3)]
            g = couple(t_nodes, tiles(n_one, index), jnp.concatenate([m_one[q] for q in index], axis=0))
            chosen = jnp.concatenate(split(l_two[uppers[t] - coarse_base]), axis=1)
            f_two = jnp.concatenate(split(lower[:, t * K : (t + 1) * K]), axis=0)
            r = dot(f_two, chosen)
            g = g + (r[:K, :R] + r[:K, R:] + r[K:, :R])
            high, low = split(g)
            g_left[t] = jnp.concatenate([high, zero, low, zero], axis=1)
            g_right[t] = jnp.concatenate([zero, high, zero, low], axis=1)

    group = near.shape[0]
    for at in range(group // 2):
        e_two = jnp.concatenate(split(transfer[:, at * 2 * K : (at + 1) * 2 * K]), axis=0)
        first = pl.program_id(0) * group + at * 2
        p_zero = parents[first] - box_base
        p_one = parents[first + 1] - box_base
        r = dot(e_two, jnp.concatenate([g_left[p_zero], g_right[p_one]], axis=0))
        g = r[:K, : 2 * R] + r[:K, 2 * R :] + r[K:, : 2 * R]
        turned = jnp.concatenate([g, g], axis=0).T
        high, low = split(turned)
        for side in range(2):
            c = at * 2 + side
            where = slice(c * B, (c + 1) * B)
            b_two = jnp.concatenate(split(basis[:, where]), axis=0)
            rows = slice(side * R, (side + 1) * R)
            f = dot(jnp.concatenate([high[rows], low[rows]], axis=0), b_two)
            out[:, where] = masked(near[c] + (f[:R] + f[R:]), counts[first + side])


def shifted(x, axis, by):
    count = lax.axis_size(axis)
    return lax.ppermute(x, axis, [(i, (i + by) % count) for i in range(count)])


def local(
    points,
    rhs,
    leaf_count,
    near_list,
    leaf_basis,
    leaf_transfer,
    leaf_parent,
    nodes1,
    box_transfer,
    box_parent,
    far1,
    nodes2,
    far2,
):
    leaves = leaf_count.shape[0]
    n_dev = lax.axis_size("dev")
    n_grp = lax.axis_size("grp")
    grp = lax.axis_index("grp")
    dev = lax.axis_index("dev")
    device = grp * n_dev + dev
    boxes = nodes1.shape[1] // K
    coarse = boxes * n_dev // CHILD
    width = REACH * B
    shape = jax.ShapeDtypeStruct

    up = [(i, i + 1) for i in range(n_dev - 1)]
    down = [(i + 1, i) for i in range(n_dev - 1)]

    def packed(side, some):
        count = jnp.broadcast_to(some.astype(F32)[:, None], (REACH, B)).reshape(1, width)
        return jnp.concatenate([rhs[:, side], points[:, side], count], axis=0)

    before = lax.ppermute(packed(slice(leaves * B - width, leaves * B), leaf_count[-REACH:]), "dev", up)
    after = lax.ppermute(packed(slice(0, width), leaf_count[:REACH]), "dev", down)

    where_am = jnp.stack([device * boxes, grp * coarse, device * leaves, dev, grp, grp * boxes * n_dev]).astype(
        jnp.int32
    )
    group = 8
    steps = leaves // group
    last = steps - 1
    table_rows = (leaves + group) * B
    listed = [
        shape((8, -(-(leaves * NEAR + UNROLL) // 128) * 128), jnp.int32),
        shape((leaves, SPAN), jnp.int32),
    ]

    def along(rows, size):
        return pl.BlockSpec((rows, size), lambda i: (0, jnp.minimum(i, last)))

    def down_rows(dims):
        return pl.BlockSpec((group, *dims), lambda i: (jnp.minimum(i, last), 0, 0))

    def whole(dims):
        return pl.BlockSpec(dims, lambda i: (0,) * len(dims))

    table, wanted, sent, *own_lists = pl.pallas_call(
        lambda *refs: upward(boxes, coarse, leaves, *refs),
        grid=(steps + 1,),
        in_specs=[
            along(3, group * B),
            along(R, group * B),
            along(K, group * B),
            along(K, group * K),
            whole(nodes1.shape),
            whole(box_transfer.shape),
            whole(near_list.shape),
            whole((1, leaves)),
        ]
        + [smem()] * 4,
        out_specs=[
            pl.BlockSpec((group * B, 2 * K), lambda i: (i, 0)),
            down_rows((K, B)),
            whole((K + 8, (boxes + coarse) * R)),
            whole(listed[0].shape),
            whole(listed[1].shape),
        ],
        out_shape=[
            shape((table_rows, 2 * K), BF16),
            shape((leaves, K, B), BF16),
            shape((K + 8, (boxes + coarse) * R), F32),
            *listed,
        ],
        scratch_shapes=[
            pltpu.VMEM((boxes, R, 2 * K), F32),
            pltpu.VMEM((boxes, R, 2 * K), F32),
            pltpu.VMEM((coarse, R, K), F32),
        ],
        compiler_params=params(),
        cost_estimate=cost(14),
        name="upward",
    )(
        points,
        rhs,
        leaf_basis,
        leaf_transfer,
        nodes1,
        box_transfer,
        near_list,
        leaf_count.reshape(1, leaves),
        leaf_count,
        leaf_parent,
        box_parent,
        where_am,
    )

    all_sent = [sent] + [shifted(sent, "dev", k) for k in range(1, n_dev)]

    buffers = [pltpu.VMEM((B, 2 * K), BF16)] * UNROLL + [pltpu.VMEM((B, B), BF16)] * (2 * UNROLL)
    near = pl.pallas_call(
        near_own,
        in_specs=[smem()] * 2 + [vmem()] * 2,
        out_specs=vmem(),
        out_shape=shape((leaves, R, B), F32),
        scratch_shapes=buffers,
        compiler_params=params(),
        cost_estimate=cost(32),
        name="near_own",
    )(*own_lists, table, wanted)

    part = all_sent[0][:K, boxes * R :]
    for other in all_sent[1:]:
        part = part + other[:K, boxes * R :]
    part, near = lax.optimization_barrier((part, near))
    tops = [part] + [shifted(part, "grp", k) for k in range(1, n_grp)]

    half = REACH // (group // 2)

    def piece(i):
        return (0, jnp.minimum(i, half - 1))

    outer, *halo_lists = pl.pallas_call(
        lambda *refs: halo_table(leaves, *refs),
        grid=(half + 1,),
        in_specs=[
            pl.BlockSpec((R + 4, group // 2 * B), piece),
            pl.BlockSpec((R + 4, group // 2 * B), piece),
            whole(near_list.shape),
            smem(),
        ],
        out_specs=[
            pl.BlockSpec((group * B, 2 * K), lambda i: (i, 0)),
            whole(listed[0].shape),
            whole(listed[1].shape),
        ],
        out_shape=[shape(((2 * REACH + group) * B, 2 * K), BF16), *listed],
        scratch_shapes=[pltpu.VMEM((8, 128), F32)],
        compiler_params=params(),
        cost_estimate=cost(5),
        name="halo_table",
    )(before, after, near_list, where_am)

    near = pl.pallas_call(
        near_halo,
        in_specs=[smem()] * 2 + [vmem()] * 3,
        out_specs=vmem(),
        out_shape=shape((leaves, R, B), F32),
        scratch_shapes=buffers,
        compiler_params=params(),
        cost_estimate=cost(12),
        name="near_halo",
    )(*halo_lists, outer, wanted, near)

    total_coarse = nodes2.shape[1] // K
    scalars = jnp.stack([where_am[q] for q in (3, 4, 0, 1, 5)])
    return pl.pallas_call(
        lambda *refs: downward(boxes, coarse, n_dev, n_grp, *refs),
        grid=(steps,),
        in_specs=[smem()] * 6
        + [whole(sent.shape)] * n_dev
        + [whole(part.shape)] * n_grp
        + [
            along(K, group * B),
            along(K, group * K),
            whole(box_transfer.shape),
            whole(nodes1.shape),
            whole(nodes2.shape),
            down_rows((R, B)),
        ],
        out_specs=along(R, group * B),
        out_shape=shape((R, leaves * B), F32),
        scratch_shapes=[
            pltpu.VMEM((boxes * n_dev, K, 2 * R), BF16),
            pltpu.VMEM((total_coarse, K, 2 * R), BF16),
            pltpu.VMEM((boxes * n_dev, 8, K), F32),
            pltpu.VMEM((total_coarse, 8, K), F32),
            pltpu.VMEM((boxes * K, 8), F32),
            pltpu.VMEM((total_coarse * K, 8), F32),
            pltpu.VMEM((coarse, K, R), F32),
            pltpu.VMEM((boxes, K, 4 * R), BF16),
            pltpu.VMEM((boxes, K, 4 * R), BF16),
        ],
        compiler_params=params(),
        cost_estimate=cost(15),
        name="downward",
    )(
        far1,
        far2,
        leaf_count,
        leaf_parent,
        box_parent,
        scalars,
        *all_sent,
        *tops,
        leaf_basis,
        leaf_transfer,
        box_transfer,
        nodes1,
        nodes2,
        near,
    )


def solution(mesh):
    placed = (
        P(None, ("grp", "dev")),
        P(None, ("grp", "dev")),
        P(("grp", "dev")),
        P(("grp", "dev"), None),
        P(None, ("grp", "dev")),
        P(None, ("grp", "dev")),
        P(("grp", "dev")),
        P(None, ("grp", "dev")),
        P(None, ("grp", "dev")),
        P(("grp", "dev")),
        P(("grp", "dev"), None),
        P(),
        P(),
    )
    return jax.shard_map(
        local, mesh=mesh, in_specs=placed, out_specs=P(None, ("grp", "dev")), check_vma=False
    )
```

time: 160 us -> 122 us (0.76); the launches traced: 157 us -> 122 us
  waiting for transfers between devices: 20.5 us -> 4.25 us
  other arithmetic: 8.99 us -> 1.26 us
  local copies, waits for them, and re-layouts: 12.8 us -> 5.76 us
  starting transfers between devices: 25.2 us -> 22.8 us
  Pallas kernels: 89.5 us -> 87.8 us
    ppermute x10, waiting for transfers between devices: 20.5 us -> 4.25 us  [shifted(): return lax.ppermute(x, axis, [(i, (i + by) % count) for i in range(count)])]
    ppermute x4 -> x2, starting transfers between devices: 12.9 us -> 6.45 us  [the longest x1 4.54 us: local(): lax.ppermute(packed(slice(0, width), leaf_count[:REACH]), 'dev', down)]
    pallas_call x1, Pallas kernels: 22.7 us -> 17.1 us  [local(): pl.pallas_call(lambda *refs: downward(boxes, coarse, n_dev, n_grp, *refs)...]
    ppermute x10, starting transfers between devices: 12.3 us -> 16.3 us  [shifted(): return lax.ppermute(x, axis, [(i, (i + by) % count) for i in range(count)])]
    pallas_call x3 -> x4, Pallas kernels: 66.8 us -> 70.7 us  [the longest x1 31.8 us: local(): pl.pallas_call(near_own, in_specs=[smem()] * 2 + [vmem()] * 2, out_specs=...]
    reduce_sum x8 -> x0, other arithmetic: 3.59 us -> none  [the longest x2 2.48 us: lists(): own = jnp.sum(jnp.where(slots[:, :, None] == known, counts, 0), axis=-1)]
    slice x4 -> x2, local copies, waits for them, and re-layouts: 3.07 us -> 0.19 us  [packed(): return jnp.concatenate([rhs[:, side], points[:, side], count], axis=0)]
    select_n x6 -> x0, other arithmetic: 2.42 us -> none  [the longest x2 2.37 us: lists(): jnp.where(t < total, at_leaf * 16 + at_chunk, (leaves - 1) * 16 + NEAR)]
  transfers between devices with their start and end apart: 14 -> 12, of which waited for: 3 -> 2; matrix products, arithmetic and copies ran while one was open for 11% -> 2% of each run, Pallas kernels for 32% -> 46%
where the time goes in v1:
time: 122 us
  Pallas kernels  87.8 us (72%)
  starting transfers between devices  22.8 us (19%)
  local copies, waits for them, and re-layouts  5.76 us (5%)
  waiting for transfers between devices  4.25 us (3%)
  other arithmetic  1.26 us (1%)
    pallas_call x1, Pallas kernels, local(): pl.pallas_call(near_own, in_specs=[smem()] * 2 + [vmem()] * 2, out_specs=...  31.8 us
    pallas_call x1, Pallas kernels, local(): pl.pallas_call(lambda *refs: downward(boxes, coarse, n_dev, n_grp, *refs)...  17.1 us
    ppermute x10, starting transfers between devices, shifted(): return lax.ppermute(x, axis, [(i, (i + by) % count) for i in range(count)])  16.3 us
    pallas_call x1, Pallas kernels, local(): pl.pallas_call(near_halo, in_specs=[smem()] * 2 + [vmem()] * 3, out_specs...  15.3 us
    pallas_call x1, Pallas kernels, local(): pl.pallas_call(lambda *refs: upward(boxes, coarse, leaves, *refs), grid=(...  15 us
    pallas_call x1, Pallas kernels, local(): pl.pallas_call(lambda *refs: halo_table(leaves, *refs), grid=(half + 1,),...  8.6 us
    ppermute x1, starting transfers between devices, local(): lax.ppermute(packed(slice(0, width), leaf_count[:REACH]), 'dev', down)  4.54 us
    unnamed x33, local copies, waits for them, and re-layouts  4.26 us
  transfers between devices with their start and end apart: 12, of which 2 were waited for; matrix products, arithmetic and copies ran while one was open for 2% of the time, Pallas kernels for 46%

profile of v1, /device:TPU:4, one launch (start us, length us, event | category | flops | bytes accessed | tf_op | source)
XLA Modules:
  0.0 122.2 jit_solution(9094674054725640718)
XLA Ops:
  0.0 1.4 %copy.14.refs_6_.refs_2_ = s32[64,8]{1,0:T(8,128)} copy(s32[64,8]{0,1:T(8,128)} %param.16) | data formatting | bytes 4096 | tf_op args[3]
  1.4 0.6 stack.31.refs_11_.refs_3_
  2.0 15.0 %upward.1 = (bf16[18432,128]{1,0:T(8,128)(2,1)}, bf16[64,64,256]{2,1,0:T(8,128)(2,1)}, f32[72,512]{1,0:T(8,128)}, s32[8,640]{1,0:T(8,128)}, s32[64,144]{1,0:T(8,128)}) custom-call(f32[3,16384]{1,0:T(4,128)} %refs_0_.2, f32[32,16384]{1,0:T(8,128)} %refs_1_.2, f32[64,16384]{1,0:T(8,128)} %refs_18_.1, f32[64,4096]{1,0:T(8,128)} %refs_19_.1, f32[3,512]{1,0:T(4,128)} %refs_21_.1, ...), custom_call_target="tpu_custom_call" | custom-call | flops 14000000000 | bytes 42000000 | tf_op jit(solution)/shard_map/upward/pallas_call | solution.py:431
  17.0 1.5 %collective-permute-start.1 = (f32[72,512]{1,0:T(8,128)}, f32[72,512]{1,0:T(8,128)S(1)}, u32[]{:S(2)}, u32[]{:S(2)}) collective-permute-start(f32[72,512]{1,0:T(8,128)} %get-tuple-element.15.refs_6_), channel_id=1, source_target_pairs={{0,2},{1,3},{2,4},{3,5},{4,6},{5,7},{6,0},{7,1},{8,10},{9,11},{10,... | collective-permute-start | bytes 442376 | tf_op jit(solution)/shard_map/ppermute | solution.py:371
  18.6 1.3 %collective-permute-start.2 = (f32[72,512]{1,0:T(8,128)}, f32[72,512]{1,0:T(8,128)S(1)}, u32[]{:S(2)}, u32[]{:S(2)}) collective-permute-start(f32[72,512]{1,0:T(8,128)} %get-tuple-element.15.refs_6_), channel_id=1, source_target_pairs={{0,3},{1,4},{2,5},{3,6},{4,7},{5,0},{6,1},{7,2},{8,11},{9,12},{10,... | collective-permute-start | bytes 442376 | tf_op jit(solution)/shard_map/ppermute | solution.py:371
  19.9 1.5 %collective-permute-start.3 = (f32[72,512]{1,0:T(8,128)}, f32[72,512]{1,0:T(8,128)S(1)}, u32[]{:S(2)}, u32[]{:S(2)}) collective-permute-start(f32[72,512]{1,0:T(8,128)} %get-tuple-element.15.refs_6_), channel_id=1, source_target_pairs={{0,4},{1,5},{2,6},{3,7},{4,0},{5,1},{6,2},{7,3},{8,12},{9,13},{10,... | collective-permute-start | bytes 442376 | tf_op jit(solution)/shard_map/ppermute | solution.py:371
  21.7 0.8 copy-done.1
  22.9 0.8 collective-permute-done.refs_7_
  23.8 1.4 %collective-permute-start.5 = (f32[72,512]{1,0:T(8,128)S(1)}, f32[72,512]{1,0:T(8,128)}, u32[]{:S(2)}, u32[]{:S(2)}) collective-permute-start(f32[72,512]{1,0:T(8,128)S(1)} %copy-done.3), channel_id=1, source_target_pairs={{0,6},{1,7},{2,0},{3,1},{4,2},{5,3},{6,4},{7,5},{8,14},{9,15},{10,... | collective-permute-start | bytes 442376 | tf_op jit(solution)/shard_map/ppermute | solution.py:371
  25.2 1.9 %collective-permute-start.6 = (f32[72,512]{1,0:T(8,128)S(1)}, f32[72,512]{1,0:T(8,128)}, u32[]{:S(2)}, u32[]{:S(2)}) collective-permute-start(f32[72,512]{1,0:T(8,128)S(1)} %copy-done.3), channel_id=1, source_target_pairs={{0,7},{1,0},{2,1},{3,2},{4,3},{5,4},{6,5},{7,6},{8,15},{9,8},{10,9... | collective-permute-start | bytes 442376 | tf_op jit(solution)/shard_map/ppermute | solution.py:371
  27.1 3.4 %collective-permute-done.2.refs_9_ = f32[72,512]{1,0:T(8,128)S(1)} collective-permute-done((f32[72,512]{1,0:T(8,128)}, f32[72,512]{1,0:T(8,128)S(1)}, u32[]{:S(2)}, u32[]{:S(2)}) %collective-permute-start.2) | collective-permute-done | bytes 147488 | tf_op jit(solution)/shard_map/ppermute | solution.py:371
  30.5 1.9 %collective-permute-start.10 = (f32[36,8192]{1,0:T(8,128)S(1)}, f32[36,8192]{1,0:T(8,128)}, u32[]{:S(2)}, u32[]{:S(2)}) collective-permute-start(f32[36,8192]{1,0:T(8,128)S(1)} %pad_maximum_fusion), channel_id=1, source_target_pairs={{0,1},{1,2},{2,3},{3,4},{4,5},{5,6},{6,7},{8,9},{9,10},{10,11},{11... | collective-permute-start | bytes 3538952 | tf_op jit(solution)/shard_map/ppermute | solution.py:407
  32.4 4.5 %collective-permute-start.11 = (f32[36,8192]{1,0:T(8,128)S(1)}, f32[36,8192]{1,0:T(8,128)}, u32[]{:S(2)}, u32[]{:S(2)}) collective-permute-start(f32[36,8192]{1,0:T(8,128)S(1)} %pad_maximum_fusion.1), channel_id=1, source_target_pairs={{1,0},{2,1},{3,2},{4,3},{5,4},{6,5},{7,6},{9,8},{10,9},{11,10},{12... | collective-permute-start | bytes 3538952 | tf_op jit(solution)/shard_map/ppermute | solution.py:408
  37.0 31.8 %near_own.1.begun = f32[64,32,256]{2,1,0:T(8,128)} custom-call(s32[8,640]{1,0:T(8,128)} %get-tuple-element.16.items, s32[64,144]{1,0:T(8,128)} %get-tuple-element.17.rows_of, bf16[18432,128]{1,0:T(8,128)(2,1)} %get-tuple-element.18.table, bf16[64,64,256]{2,1,0:T(8,128)(2,1)} %get-tuple-element.19.wanted), custom_call_target="tpu_custom_call" | custom-call | flops 32000000000 | bytes 96000000 | tf_op jit(solution)/shard_map/near_own/pallas_call | solution.py:484
  68.8 0.7 stack.29.refs_5_
  69.5 0.7 copy.16.refs_1_
  70.2 0.9 slice_add_fusion.refs_14_
  71.2 2.4 %collective-permute-start.7 = (f32[64,256]{1,0:T(8,128)S(1)}, f32[64,256]{1,0:T(8,128)S(1)}, u32[]{:S(2)}, u32[]{:S(2)}) collective-permute-start(f32[64,256]{1,0:T(8,128)S(1)} %slice_add_fusion.refs_14_), channel_id=1, source_target_pairs={{0,8},{8,16},{16,24},{24,0},{1,9},{9,17},{17,25},{25,1},{2,10},{10... | collective-permute-start | bytes 196616 | tf_op jit(solution)/shard_map/ppermute | solution.py:371
  73.5 3.3 %collective-permute-start.8 = (f32[64,256]{1,0:T(8,128)S(1)}, f32[64,256]{1,0:T(8,128)S(1)}, u32[]{:S(2)}, u32[]{:S(2)}) collective-permute-start(f32[64,256]{1,0:T(8,128)S(1)} %slice_add_fusion.refs_14_), channel_id=1, source_target_pairs={{0,16},{8,24},{16,0},{24,8},{1,17},{9,25},{17,1},{25,9},{2,18},{10... | collective-permute-start | bytes 196616 | tf_op jit(solution)/shard_map/ppermute | solution.py:371
  76.9 2.8 %collective-permute-start.9 = (f32[64,256]{1,0:T(8,128)S(1)}, f32[64,256]{1,0:T(8,128)S(1)}, u32[]{:S(2)}, u32[]{:S(2)}) collective-permute-start(f32[64,256]{1,0:T(8,128)S(1)} %slice_add_fusion.refs_14_), channel_id=1, source_target_pairs={{0,24},{8,0},{16,8},{24,16},{1,25},{9,1},{17,9},{25,17},{2,26},{10... | collective-permute-start | bytes 196616 | tf_op jit(solution)/shard_map/ppermute | solution.py:371
  79.8 8.6 %halo_table.1 = (bf16[18432,128]{1,0:T(8,128)(2,1)}, s32[8,640]{1,0:T(8,128)}, s32[64,144]{1,0:T(8,128)}) custom-call(f32[36,8192]{1,0:T(8,128)} %collective-permute-done.10.refs_0_, f32[36,8192]{1,0:T(8,128)} %collective-permute-done.11.refs_1_, s32[64,8]{1,0:T(8,128)} %copy.14.refs_6_.refs_2_, s32[6]{0:T(128)} %stack.31.refs_11_.refs_3_), custom_call_target="tpu_custom_call" | custom-call | flops 5000000000 | bytes 15000000 | tf_op jit(solution)/shard_map/halo_table/pallas_call | solution.py:506
  88.4 15.3 %near_halo.1.refs_23_ = f32[64,32,256]{2,1,0:T(8,128)} custom-call(s32[8,640]{1,0:T(8,128)} %get-tuple-element.21.items, s32[64,144]{1,0:T(8,128)} %get-tuple-element.22.rows_of, bf16[18432,128]{1,0:T(8,128)(2,1)} %get-tuple-element.23.table, bf16[64,64,256]{2,1,0:T(8,128)(2,1)} %get-tuple-element.19.wanted, f32[64,32,256]{2,1,0:T(8,128)} %near_own.1.begun), custom_call_target="tpu_custom_call" | custom-call | flops 12000000000 | bytes 36000000 | tf_op jit(solution)/shard_map/near_halo/pallas_call | solution.py:527
  104.3 0.6 copy-done.13
  104.9 17.1 %downward.1 = f32[32,16384]{1,0:T(8,128)} custom-call(s32[8,16]{1,0:T(8,128)} %refs_0_.3, s32[32,8]{1,0:T(8,128)} %copy.16.refs_1_, s32[64]{0:T(128)} %refs_2_.4, s32[64]{0:T(128)} %refs_3_.3, s32[8]{0:T(128)} %refs_4_.3, s32[5]{0:T(128)} %stack.29.refs_5_, f32[72,512]{1,0:T(8,128)} %get-tuple-element.15.refs_6_, f32[72,512]{1,0:T(8,128)} %copy-done.4, ...), custom_call_target="tpu_custom_call" | custom-call | flops 15000000512 | bytes 45000000 | tf_op jit(solution)/shard_map/downward/pallas_call | solution.py:540
  (46 shorter events, 1.4 us)
Async XLA Ops:
  2.0 19.4 %copy-start.10 = (s32[64]{0:T(128)S(1)}, s32[64]{0:T(128)}, u32[]{:S(2)}) copy-start(s32[64]{0:T(128)} %refs_2_.4) | copy-start | bytes 772
  2.0 19.5 %copy-start = (f32[32,16384]{1,0:T(8,128)S(1)}, f32[32,16384]{1,0:T(8,128)}, u32[]{:S(2)}) copy-start(f32[32,16384]{1,0:T(8,128)} %refs_1_.2) | copy-start | bytes 6291460
  17.0 6.8 %collective-permute-start = (f32[72,512]{1,0:T(8,128)}, f32[72,512]{1,0:T(8,128)S(1)}, u32[]{:S(2)}, u32[]{:S(2)}) collective-permute-start(f32[72,512]{1,0:T(8,128)} %get-tuple-element.15.refs_6_), channel_id=1, source_target_pairs={{0,1},{1,2},{2,3},{3,4},{4,5},{5,6},{6,7},{7,0},{8,9},{9,10},{10,1... | collective-permute-start | bytes 442376 | tf_op jit(solution)/shard_map/ppermute | solution.py:371
  17.0 8.1 %collective-permute-start.1 = (f32[72,512]{1,0:T(8,128)}, f32[72,512]{1,0:T(8,128)S(1)}, u32[]{:S(2)}, u32[]{:S(2)}) collective-permute-start(f32[72,512]{1,0:T(8,128)} %get-tuple-element.15.refs_6_), channel_id=1, source_target_pairs={{0,2},{1,3},{2,4},{3,5},{4,6},{5,7},{6,0},{7,1},{8,10},{9,11},{10,... | collective-permute-start | bytes 442376 | tf_op jit(solution)/shard_map/ppermute | solution.py:371
  18.6 11.9 %collective-permute-start.2 = (f32[72,512]{1,0:T(8,128)}, f32[72,512]{1,0:T(8,128)S(1)}, u32[]{:S(2)}, u32[]{:S(2)}) collective-permute-start(f32[72,512]{1,0:T(8,128)} %get-tuple-element.15.refs_6_), channel_id=1, source_target_pairs={{0,3},{1,4},{2,5},{3,6},{4,7},{5,0},{6,1},{7,2},{8,11},{9,12},{10,... | collective-permute-start | bytes 442376 | tf_op jit(solution)/shard_map/ppermute | solution.py:371
  19.9 12.5 %collective-permute-start.3 = (f32[72,512]{1,0:T(8,128)}, f32[72,512]{1,0:T(8,128)S(1)}, u32[]{:S(2)}, u32[]{:S(2)}) collective-permute-start(f32[72,512]{1,0:T(8,128)} %get-tuple-element.15.refs_6_), channel_id=1, source_target_pairs={{0,4},{1,5},{2,6},{3,7},{4,0},{5,1},{6,2},{7,3},{8,12},{9,13},{10,... | collective-permute-start | bytes 442376 | tf_op jit(solution)/shard_map/ppermute | solution.py:371
  21.4 48.7 %collective-permute-start.4 = (f32[72,512]{1,0:T(8,128)}, f32[72,512]{1,0:T(8,128)S(1)}, u32[]{:S(2)}, u32[]{:S(2)}) collective-permute-start(f32[72,512]{1,0:T(8,128)} %get-tuple-element.15.refs_6_), channel_id=1, source_target_pairs={{0,5},{1,6},{2,7},{3,0},{4,1},{5,2},{6,3},{7,4},{8,13},{9,14},{10,... | collective-permute-start | bytes 442376 | tf_op jit(solution)/shard_map/ppermute | solution.py:371
  21.5 1.0 copy-start.1
  22.8 1.0 copy-start.3
  23.8 46.4 %copy-start.4 = (f32[72,512]{1,0:T(8,128)}, f32[72,512]{1,0:T(8,128)S(1)}, u32[]{:S(2)}) copy-start(f32[72,512]{1,0:T(8,128)S(1)} %collective-permute-done.refs_7_) | copy-start | bytes 442372
  23.8 46.4 %collective-permute-start.5 = (f32[72,512]{1,0:T(8,128)S(1)}, f32[72,512]{1,0:T(8,128)}, u32[]{:S(2)}, u32[]{:S(2)}) collective-permute-start(f32[72,512]{1,0:T(8,128)S(1)} %copy-done.3), channel_id=1, source_target_pairs={{0,6},{1,7},{2,0},{3,1},{4,2},{5,3},{6,4},{7,5},{8,14},{9,15},{10,... | collective-permute-start | bytes 442376 | tf_op jit(solution)/shard_map/ppermute | solution.py:371
  25.2 45.1 %copy-start.5 = (f32[72,512]{1,0:T(8,128)}, f32[72,512]{1,0:T(8,128)S(1)}, u32[]{:S(2)}) copy-start(f32[72,512]{1,0:T(8,128)S(1)} %collective-permute-done.1.refs_8_) | copy-start | bytes 442372
  25.2 45.0 %collective-permute-start.6 = (f32[72,512]{1,0:T(8,128)S(1)}, f32[72,512]{1,0:T(8,128)}, u32[]{:S(2)}, u32[]{:S(2)}) collective-permute-start(f32[72,512]{1,0:T(8,128)S(1)} %copy-done.3), channel_id=1, source_target_pairs={{0,7},{1,0},{2,1},{3,2},{4,3},{5,4},{6,5},{7,6},{8,15},{9,8},{10,9... | collective-permute-start | bytes 442376 | tf_op jit(solution)/shard_map/ppermute | solution.py:371
  30.5 39.7 %copy-start.6 = (f32[72,512]{1,0:T(8,128)}, f32[72,512]{1,0:T(8,128)S(1)}, u32[]{:S(2)}) copy-start(f32[72,512]{1,0:T(8,128)S(1)} %collective-permute-done.2.refs_9_) | copy-start | bytes 442372
  30.5 49.3 %collective-permute-start.10 = (f32[36,8192]{1,0:T(8,128)S(1)}, f32[36,8192]{1,0:T(8,128)}, u32[]{:S(2)}, u32[]{:S(2)}) collective-permute-start(f32[36,8192]{1,0:T(8,128)S(1)} %pad_maximum_fusion), channel_id=1, source_target_pairs={{0,1},{1,2},{2,3},{3,4},{4,5},{5,6},{6,7},{8,9},{9,10},{10,11},{11... | collective-permute-start | bytes 3538952 | tf_op jit(solution)/shard_map/ppermute | solution.py:407
  32.4 37.8 %copy-start.7 = (f32[72,512]{1,0:T(8,128)}, f32[72,512]{1,0:T(8,128)S(1)}, u32[]{:S(2)}) copy-start(f32[72,512]{1,0:T(8,128)S(1)} %collective-permute-done.3.refs_10_) | copy-start | bytes 442372
  32.4 47.3 %collective-permute-start.11 = (f32[36,8192]{1,0:T(8,128)S(1)}, f32[36,8192]{1,0:T(8,128)}, u32[]{:S(2)}, u32[]{:S(2)}) collective-permute-start(f32[36,8192]{1,0:T(8,128)S(1)} %pad_maximum_fusion.1), channel_id=1, source_target_pairs={{1,0},{2,1},{3,2},{4,3},{5,4},{6,5},{7,6},{9,8},{10,9},{11,10},{12... | collective-permute-start | bytes 3538952 | tf_op jit(solution)/shard_map/ppermute | solution.py:408
  37.0 32.5 %copy-start.9 = (s32[32,8]{0,1:T(8,128)S(1)}, s32[32,8]{0,1:T(8,128)}, u32[]{:S(2)}) copy-start(s32[32,8]{0,1:T(8,128)} %param.25) | copy-start | bytes 3076
  70.2 18.2 %copy-start.8 = (f32[72,512]{1,0:T(8,128)}, f32[72,512]{1,0:T(8,128)S(1)}, u32[]{:S(2)}) copy-start(f32[72,512]{1,0:T(8,128)S(1)} %collective-permute-done.4.refs_11_) | copy-start | bytes 442372
  71.2 17.2 %copy-start.2 = (f32[64,256]{1,0:T(8,128)}, f32[64,256]{1,0:T(8,128)S(1)}, u32[]{:S(2)}) copy-start(f32[64,256]{1,0:T(8,128)S(1)} %slice_add_fusion.refs_14_) | copy-start | bytes 196612
  71.2 32.5 %collective-permute-start.7 = (f32[64,256]{1,0:T(8,128)S(1)}, f32[64,256]{1,0:T(8,128)S(1)}, u32[]{:S(2)}, u32[]{:S(2)}) collective-permute-start(f32[64,256]{1,0:T(8,128)S(1)} %slice_add_fusion.refs_14_), channel_id=1, source_target_pairs={{0,8},{8,16},{16,24},{24,0},{1,9},{9,17},{17,25},{25,1},{2,10},{10... | collective-permute-start | bytes 196616 | tf_op jit(solution)/shard_map/ppermute | solution.py:371
  73.5 30.1 %collective-permute-start.8 = (f32[64,256]{1,0:T(8,128)S(1)}, f32[64,256]{1,0:T(8,128)S(1)}, u32[]{:S(2)}, u32[]{:S(2)}) collective-permute-start(f32[64,256]{1,0:T(8,128)S(1)} %slice_add_fusion.refs_14_), channel_id=1, source_target_pairs={{0,16},{8,24},{16,0},{24,8},{1,17},{9,25},{17,1},{25,9},{2,18},{10... | collective-permute-start | bytes 196616 | tf_op jit(solution)/shard_map/ppermute | solution.py:371
  76.9 26.8 %collective-permute-start.9 = (f32[64,256]{1,0:T(8,128)S(1)}, f32[64,256]{1,0:T(8,128)S(1)}, u32[]{:S(2)}, u32[]{:S(2)}) collective-permute-start(f32[64,256]{1,0:T(8,128)S(1)} %slice_add_fusion.refs_14_), channel_id=1, source_target_pairs={{0,24},{8,0},{16,8},{24,16},{1,25},{9,1},{17,9},{25,17},{2,26},{10... | collective-permute-start | bytes 196616 | tf_op jit(solution)/shard_map/ppermute | solution.py:371
  103.7 0.6 copy-start.12
  (2 other events, 1.2 us)
